TPU v7x, 512 devices: a whole 4x4x16 slice. The times are simulated.
512 devices in a mesh: row: 16 (over z_lo, x), col: 32 (over z_hi, y, core).
Axes of the slice: x: 4, y: 4, z: 16 (z_hi: 4, z_lo: 4; z = z_hi * 4 + z_lo), core: 2. Of those that a mesh axis runs over, the one named last changes fastest.
Arguments:
- b_diag: float32 [512, 512], P('row'), as said below
- a_diag: float32 [512, 512], P('row'), as said below
- b_panel: float32 [16384, 512], P(('row', 'col')), may hold values from -2 to 2
- a_panel: float32 [16384, 512], P(('row', 'col')), may hold values from -2 to 2
- a_trail: float32 [16384, 16384], P('row', 'col'), as said below
Outputs:
- a_diag_new: float32 [512, 512], P('row')
- l_panel: float32 [16384, 512], P(('row', 'col'))
- a_panel_new: float32 [16384, 512], P(('row', 'col'))
- a_trail_new: float32 [16384, 16384], P('row', 'col')
Inputs may be any that keep to these rules, and one draw needn't show every extreme that they name: b_diag is symmetric positive definite, its smallest eigenvalue 0.5 or more. a_diag is symmetric. a_trail is symmetric.
All inputs are finite; a program needn't handle non-finite values.
Results may differ from a plain program's by a relative error of at most 0.0001.
Values sent between devices are 32-bit elements; how exact they have to be, the bound alone decides.
A program may use at most 64 MiB of HBM per device.

v0:
```python
import jax
import jax.numpy as jnp
from jax import lax
from jax.sharding import Mesh
from jax.sharding import PartitionSpec as P

ROW = ("row_0", "row_1")
ROW_COL = ("row_0", "row_1", "col")
HIGHEST = lax.Precision.HIGHEST


def in_order(pieces, dim):
    pieces = jnp.moveaxis(pieces, 0, dim)
    lengths = pieces.shape
    return pieces.reshape(*lengths[:dim], lengths[dim] * lengths[dim + 1], *lengths[dim + 2 :])


def from_everyone(array, axis):
    copies = jnp.broadcast_to(array, (lax.axis_size(axis), *array.shape))
    return lax.all_to_all(copies, axis, split_axis=0, concat_axis=0, tiled=True)


def gathered_copies(array, axis, dim):
    return in_order(from_everyone(array, axis), dim)


def gather_in_order(array, axes, order):
    pieces = array[None]
    for k in order:
        pieces = lax.all_gather(pieces, axes[k], axis=0, tiled=True)
    block = [lax.axis_size(axes[k]) for k in reversed(order)]
    pieces = pieces.reshape(*block, *array.shape)
    turned = sorted(range(len(order)), key=lambda place: order[len(order) - 1 - place])
    return pieces.transpose(*turned, *range(len(order), pieces.ndim)).reshape(-1, *array.shape)


def gather_axes(array, axes, order, dim):
    return in_order(gather_in_order(array, axes, order), dim)


def sent_together(arrays, axis, dim, along):
    ends, at = ([], 0)
    for a in arrays[:-1]:
        at += a.shape[along]
        ends.append(at)
    both = jnp.concatenate(arrays, axis=along)
    return tuple(jnp.split(lax.all_gather(both, axis, axis=dim, tiled=True), ends, axis=along))


def spread(array, axis, root):
    mine = lax.axis_index(axis) == root
    return lax.psum(jnp.where(mine, array, jnp.zeros_like(array)), axis)


def matmul(left, right):
    return jnp.dot(left, right, precision=HIGHEST, preferred_element_type=jnp.float32)


def outer_sum(left, right):
    return lax.dot_general(
        left, right, (((1,), (1,)), ((), ())), precision=HIGHEST, preferred_element_type=jnp.float32
    )


def invert_factor(b_full):
    factor = jnp.linalg.cholesky(b_full)
    identity = jnp.eye(b_full.shape[0], dtype=b_full.dtype)
    return jax.scipy.linalg.solve_triangular(factor, identity, lower=True)


def shards(b_diag, a_diag, b_panel, a_panel, a_trail):
    piece_rows = a_diag.shape[0]
    b_full = gathered_copies(b_diag, ROW, 0)
    inverse = invert_factor(b_full)
    right_piece = matmul(a_diag, inverse.T)
    right_full = gather_axes(right_piece, ROW, (0, 1), 0)
    a_diag_full = matmul(inverse, right_full)
    grid_row = lax.axis_index(ROW)
    a_diag_new = lax.dynamic_slice_in_dim(a_diag_full, grid_row * piece_rows, piece_rows, 0)
    l_panel = matmul(b_panel, inverse.T)
    correction = 0.5 * matmul(l_panel, a_diag_full)
    mixed = matmul(a_panel, inverse.T) - correction
    a_panel_new = mixed - correction
    row_factor, row_mixed = sent_together((l_panel, mixed), "col", 0, 1)
    height = a_trail.shape[0]
    width_cols = a_trail.shape[1]
    grid_col = lax.axis_index("col")
    source_row = grid_col * width_cols // height
    start = jnp.clip(grid_col * width_cols - grid_row * height, 0, height - width_cols)
    outgoing = (
        lax.dynamic_slice_in_dim(row_factor, start, width_cols, 0),
        lax.dynamic_slice_in_dim(row_mixed, start, width_cols, 0),
    )
    col_factor, col_mixed = (
        spread(outgoing[0], ROW, source_row),
        spread(outgoing[1], ROW, source_row),
    )
    a_trail_new = a_trail - outer_sum(row_mixed, col_factor) - outer_sum(row_factor, col_mixed)
    return (a_diag_new, l_panel, a_panel_new, a_trail_new)


def solution(mesh):
    split = Mesh(mesh.devices.reshape(4, 4, mesh.shape["col"]), ("row_0", "row_1", "col"))
    return jax.shard_map(
        shards,
        mesh=split,
        in_specs=(P(ROW, None), P(ROW, None), P(ROW_COL, None), P(ROW_COL, None), P(ROW, "col")),
        out_specs=(P(ROW, None), P(ROW_COL, None), P(ROW_COL, None), P(ROW, "col")),
        check_vma=False,
    )
```

profile of v0, /device:TPU:8, one launch (start us, length us, event | category | flops | bytes accessed | tf_op | source)
XLA Modules:
  0.0 533.0 jit_solution(2031386575050240520)
XLA Ops:
  7.2 2.0 broadcast_in_dim.8
  9.1 8.5 %all-to-all-start = ((f32[16,32,512]{2,1,0:T(8,128)}), f32[16,32,512]{2,1,0:T(8,128)S(1)}, u32[]{:S(2)}, u32[]{:S(2)}) async-start(f32[16,32,512]{2,1,0:T(8,128)} %broadcast_in_dim.8), calls=%async_computation | async-start | bytes 2097152 | tf_op jit(solution)/shard_map/all_to_all | solution.py:20
  17.7 0.1 iota_compare_fusion
  17.8 0.1 fusion.10
  17.9 24.3 %all-to-all-done = f32[16,32,512]{2,1,0:T(8,128)S(1)} async-done(((f32[16,32,512]{2,1,0:T(8,128)}), f32[16,32,512]{2,1,0:T(8,128)S(1)}, u32[]{:S(2)}, u32[]{:S(2)}) %all-to-all-start) | async-done | bytes 1048608 | tf_op jit(solution)/shard_map/all_to_all | solution.py:20
  42.2 0.3 copy.14
  42.6 0.2 fusion.1
  42.8 1.0 copy-done.2
  43.8 11.7 %cholesky.104 = f32[128,128]{1,0:T(8,128)S(1)} custom-call(f32[128,128]{1,0:T(8,128)S(1)} %cholesky.266), custom_call_target="Cholesky" | custom-call | tf_op jit(solution)/shard_map/jit(cholesky)/cholesky | solution.py:66
  55.6 9.8 %custom-call.31 = f32[1,128,128]{1,2,0:T(8,128)S(1)} custom-call(f32[1,128,128]{2,1,0:T(8,128)S(1)} %get-tuple-element.35), custom_call_target="InvertDiagBlocksLowerTriangular" | custom-call | tf_op jit(solution)/shard_map/jit(cholesky)/cholesky | solution.py:66
  65.4 0.1 cholesky.224
  65.5 1.2 constant_dynamic-update-slice_fusion.1
  66.7 1.3 convolution_subtract_fusion.3
  68.0 11.7 %cholesky.217 = f32[128,128]{1,0:T(8,128)S(1)} custom-call(f32[128,128]{1,0:T(8,128)S(1)} %cholesky.270), custom_call_target="Cholesky" | custom-call | tf_op jit(solution)/shard_map/jit(cholesky)/cholesky | solution.py:66
  79.8 10.3 %custom-call.32 = f32[1,128,128]{1,2,0:T(8,128)S(1)} custom-call(f32[1,128,128]{2,1,0:T(8,128)S(1)} %get-tuple-element.32), custom_call_target="InvertDiagBlocksLowerTriangular" | custom-call | tf_op jit(solution)/shard_map/jit(cholesky)/cholesky | solution.py:66
  90.0 0.3 convolution_dynamic-update-slice_fusion
  90.3 1.3 convolution_subtract_fusion.4
  91.6 11.7 %cholesky.238 = f32[128,128]{1,0:T(8,128)S(1)} custom-call(f32[128,128]{1,0:T(8,128)S(1)} %cholesky.275), custom_call_target="Cholesky" | custom-call | tf_op jit(solution)/shard_map/jit(cholesky)/cholesky | solution.py:66
  103.4 0.7 compare_reduce_fusion.1
  104.0 9.8 %custom-call.33 = f32[1,128,128]{1,2,0:T(8,128)S(1)} custom-call(f32[1,128,128]{2,1,0:T(8,128)S(1)} %get-tuple-element.29), custom_call_target="InvertDiagBlocksLowerTriangular" | custom-call | tf_op jit(solution)/shard_map/jit(cholesky)/cholesky | solution.py:66
  113.8 0.2 convolution_dynamic-update-slice_fusion.1
  114.0 1.2 convolution_subtract_fusion.5
  115.3 11.7 %cholesky.255 = f32[128,128]{1,0:T(8,128)S(1)} custom-call(f32[128,128]{1,0:T(8,128)S(1)} %convolution_subtract_fusion.5), custom_call_target="Cholesky" | custom-call | tf_op jit(solution)/shard_map/jit(cholesky)/cholesky | solution.py:66
  127.0 0.8 compare_reduce_fusion
  127.8 0.6 compare_reduce_fusion.2
  131.0 0.1 select_select_fusion
  131.2 10.4 %while.1 = (s32[]{:T(128)}, f32[512,512]{1,0:T(8,128)S(1)}, s32[4,2]{0,1:T(2,128)S(1)}, f32[4,128,128]{2,1,0:T(8,128)}, s32[]{:T(128)}) while((s32[]{:T(128)}, f32[512,512]{1,0:T(8,128)S(1)}, s32[4,2]{0,1:T(2,128)S(1)}, f32[4,128,128]{2,1,0:T(8,128)}, s32[]{:T(128)}) %tuple.33), condition=%wide.while_cond, body=%wide.while_body.sunk | while | flops 2 | bytes 132205 | solution.py:68
  131.2 0.1 constant_dynamic-slice_fusion.3
  131.2 0.5 fusion.54
  131.8 2.0 bitcast_dynamic-update-slice_fusion.2
  133.8 0.1 constant_dynamic-slice_fusion.3
  133.8 0.5 fusion.54
  134.4 2.0 bitcast_dynamic-update-slice_fusion.2
  136.4 0.1 constant_dynamic-slice_fusion.3
  136.4 0.5 fusion.54
  137.0 2.0 bitcast_dynamic-update-slice_fusion.2
  139.1 0.5 fusion.54
  139.6 2.0 bitcast_dynamic-update-slice_fusion.2
  141.6 40.1 %custom-call.34 = f32[4,128,128]{1,2,0:T(8,128)S(1)} custom-call(f32[4,128,128]{2,1,0:T(8,128)} %get-tuple-element.11), custom_call_target="InvertDiagBlocksLowerTriangular" | custom-call | tf_op jit(solution)/shard_map/jit(_solve_triangular)/triangular_solve | solution.py:68
  181.7 0.3 fusion.12
  182.1 0.4 convolution_subtract_fusion.1
  182.4 0.4 fusion.24
  182.9 0.4 convolution_subtract_fusion
  183.3 0.4 fusion.22
  183.8 0.6 convolution_subtract_fusion.2
  184.4 1.3 fusion.21
  185.7 1.1 convolution_bitcast_fusion.1
  186.7 16.5 %all-gather = f32[128,512]{1,0:T(8,128)} all-gather(f32[32,512]{1,0:T(8,128)S(1)} %convolution_bitcast_fusion.1), channel_id=2, replica_groups=mesh['row_0'=4,'row_1'=4,'col'=32] {'row_0'}, dimensions={0}, use_global_device_ids=true | all-gather | bytes 327680 | tf_op jit(solution)/shard_map/all_gather | solution.py:30
  203.4 1.1 fusion.35
  204.5 30.4 %all-gather.4.cloned.1.call-done = f32[16,32,512]{2,1,0:T(8,128)} async-done(((f32[4,32,512]{2,1,0:T(8,128)}), f32[16,32,512]{2,1,0:T(8,128)}) %all-gather.4.cloned.1.call-update) | async-done | bytes 1048592 | tf_op jit(solution)/shard_map/all_gather | solution.py:30
  234.9 1.3 copy.15
  236.2 1.9 fusion.36
  238.1 0.7 convolution_multiply_fusion
  238.8 1.7 fusion.39
  240.5 0.7 pad_maximum_fusion.1
  241.2 0.3 all-reduce.4.cloned.1.call-start
  241.5 95.3 %all-gather.6.cloned.1.call-done = f32[1024,1024]{1,0:T(8,128)} async-done(((f32[32,1024]{1,0:T(8,128)}), f32[1024,1024]{1,0:T(8,128)}) %all-gather.6.cloned.1.call-update) | async-done | bytes 4194320 | tf_op jit(solution)/shard_map/all_gather | solution.py:47
  336.8 2.7 fusion.38
  339.5 1.2 dynamic-slice_select_fusion
  340.6 1.1 dynamic-slice_select_fusion.1
  341.8 0.6 constant_dynamic-slice_fusion.1
  342.4 173.4 %all-reduce.4.cloned.1.call-done = (f32[512,512]{1,0:T(8,128)}, f32[512,512]{1,0:T(8,128)}) async-done(((f32[512,512]{1,0:T(8,128)}, f32[512,512]{1,0:T(8,128)}), (f32[512,512]{1,0:T(8,128)}, f32[512,512]{1,0:T(8,128)})) %all-reduce.4.cloned.1.call-update) | async-done | bytes 2097168 | tf_op jit(solution)/shard_map/psum | solution.py:52
  515.8 5.5 %fusion.33 = f32[1024,512]{1,0:T(8,128)S(1)} fusion(f32[512,512]{1,0:T(8,128)} %get-tuple-element.20, f32[1024,1024]{1,0:T(8,128)} %all-gather.6.cloned.1.call-done), kind=kOutput, calls=%fused_computation.78 | convolution fusion | flops 3221225472 | bytes 5242880 | tf_op jit(solution)/shard_map/dot_general | solution.py:60
  521.3 5.0 subtract_subtract_fusion
  (33 shorter events, 0.4 us)
Async XLA Ops:
  7.2 231.6 %copy-start = (f32[32,512]{1,0:T(8,128)S(1)}, f32[32,512]{1,0:T(8,128)}, u32[]{:S(2)}) copy-start(f32[32,512]{1,0:T(8,128)} %param.8) | copy-start | bytes 196612
  9.1 33.1 %all-to-all-start = ((f32[16,32,512]{2,1,0:T(8,128)}), f32[16,32,512]{2,1,0:T(8,128)S(1)}, u32[]{:S(2)}, u32[]{:S(2)}) async-start(f32[16,32,512]{2,1,0:T(8,128)} %broadcast_in_dim.8), calls=%async_computation | async-start | bytes 2097152 | tf_op jit(solution)/shard_map/all_to_all | solution.py:20
  17.6 217.3 %all-gather.4.cloned.1.call-start = ((), (), s32[]{:S(2)}) async-start(), calls=%async_computation.1 | async-start | bytes 1310720 | tf_op jit(solution)/shard_map/all_gather | solution.py:30
  42.8 1.0 copy-start.2
  181.7 1.6 copy-start.5
  182.4 3.2 copy-start.7
  183.7 19.6 %copy-start.8 = (f32[32,512]{1,0:T(8,128)S(1)}, f32[32,512]{1,0:T(8,128)}, u32[]{:S(2)}) copy-start(f32[32,512]{1,0:T(8,128)} %param.7) | copy-start | bytes 196612
  203.3 133.5 %all-gather.6.cloned.1.call-start = ((), (), s32[]{:S(2)}) async-start(), calls=%async_computation.2 | async-start | bytes 4325376 | tf_op jit(solution)/shard_map/all_gather | solution.py:47
  204.4 36.0 %copy-start.6 = (f32[512,32]{0,1:T(8,128)}, f32[512,32]{0,1:T(8,128)S(1)}, u32[]{:S(2)}) copy-start(f32[512,32]{0,1:T(8,128)S(1)} %fusion.35) | copy-start | bytes 196612
  241.2 274.6 %all-reduce.4.cloned.1.call-start = ((), (), s32[]{:S(2)}) async-start(), calls=%async_computation.3 | async-start | bytes 4194304 | tf_op jit(solution)/shard_map/psum | solution.py:52
  341.7 179.5 %copy-start.3 = (f32[1024,512]{1,0:T(8,128)S(1)}, f32[1024,512]{1,0:T(8,128)}, u32[]{:S(2)}) copy-start(f32[1024,512]{1,0:T(8,128)} %param.9) | copy-start | bytes 6291460
  515.8 5.5 %copy-start.1 = (f32[1024,1024]{1,0:T(8,128)S(1)}, f32[1024,1024]{1,0:T(8,128)}, u32[]{:S(2)}) copy-start(f32[1024,1024]{1,0:T(8,128)} %all-gather.6.cloned.1.call-done) | copy-start | bytes 12582916
  515.8 5.5 %copy-start.4 = (f32[512,512]{1,0:T(8,128)S(1)}, f32[512,512]{1,0:T(8,128)}, u32[]{:S(2)}) copy-start(f32[512,512]{1,0:T(8,128)} %get-tuple-element.21) | copy-start | bytes 3145732
Sparse Core Ops, SparseCore 0:
  203.4 31.4 all-gather.3
  241.3 95.4 all-gather.5
  341.9 173.8 all-reduce.3
where the time goes:
time: 542 us; the launch traced here: 533 us
  waiting for transfers between devices  324 us (60%)
  other arithmetic  123 us (23%)
  matrix products  26.2 us (5%)
  local copies, waits for them, and re-layouts  18.5 us (3%)
  between operations  17 us (3%)
  blocking collectives  16.5 us (3%)
  starting transfers between devices  8.8 us (2%)
    psum x1, waiting for transfers between devices, spread(): return lax.psum(jnp.where(mine, array, jnp.zeros_like(array)), axis)  173 us
    all_gather x1, waiting for transfers between devices, sent_together(): lax.all_gather(both, axis, axis=dim, tiled=True)  95.3 us
    another operation x14, other arithmetic, invert_factor(): factor = jnp.linalg.cholesky(b_full)  78.9 us
    another operation x3, other arithmetic, invert_factor(): return jax.scipy.linalg.solve_triangular(factor, identity, lower=True)  40.3 us
    all_gather x1, waiting for transfers between devices, gather_in_order(): pieces = lax.all_gather(pieces, axes[k], axis=0, tiled=True)  30.4 us
    all_to_all x1, waiting for transfers between devices, from_everyone(): return lax.all_to_all(copies, axis, split_axis=0, concat_axis=0, tiled=True)  24.3 us
    all_gather x1, blocking collectives, gather_in_order(): pieces = lax.all_gather(pieces, axes[k], axis=0, tiled=True)  16.5 us
  transfers between devices with their start and end apart: 4, of which 4 were waited for; matrix products, arithmetic and copies ran while one was open for 0% of the time, Pallas kernels for 0%

commit v1 on v0

--- a/solution.py
+++ b/solution.py
@@ -27,7 +27,9 @@
 def gather_in_order(array, axes, order):
     pieces = array[None]
     for k in order:
-        pieces = lax.all_gather(pieces, axes[k], axis=0, tiled=True)
+        pieces = jnp.concatenate(
+            lax.all_to_all(jnp.stack([pieces] * lax.axis_size(axes[k])), axes[k], 0, 0), axis=0
+        )
     block = [lax.axis_size(axes[k]) for k in reversed(order)]
     pieces = pieces.reshape(*block, *array.shape)
     turned = sorted(range(len(order)), key=lambda place: order[len(order) - 1 - place])

time: 542 us -> 523 us (0.965)
  waiting for transfers between devices: 324 us -> 304 us
    all_gather x1 -> x0, waiting for transfers between devices: 30.4 us -> none  [gather_in_order(): pieces = lax.all_gather(pieces, axes[k], axis=0, tiled=True)]
    all_gather x1 -> x0, blocking collectives: 16.5 us -> none  [gather_in_order(): pieces = lax.all_gather(pieces, axes[k], axis=0, tiled=True)]
    all_to_all x0 -> x1, blocking collectives: none -> 13 us  [gather_in_order(): lax.all_to_all(jnp.stack([pieces] * lax.axis_size(axes[k])), axes[k], 0, 0)]
    all_to_all x0 -> x1, waiting for transfers between devices: none -> 11.1 us  [gather_in_order(): lax.all_to_all(jnp.stack([pieces] * lax.axis_size(axes[k])), axes[k], 0, 0)]
    another operation x12 -> x14, local copies, waits for them, and re-layouts: 10.4 us -> 11.5 us
where the time goes in v1:
time: 523 us; the launch traced here: 514 us
  waiting for transfers between devices  304 us (58%)
  other arithmetic  123 us (24%)
  matrix products  26.2 us (5%)
  local copies, waits for them, and re-layouts  18.4 us (4%)
  between operations  17.2 us (3%)
  blocking collectives  13 us (2%)
  starting transfers between devices  12.3 us (2%)
    psum x1, waiting for transfers between devices, spread(): return lax.psum(jnp.where(mine, array, jnp.zeros_like(array)), axis)  173 us
    all_gather x1, waiting for transfers between devices, sent_together(): lax.all_gather(both, axis, axis=dim, tiled=True)  95.5 us
    another operation x14, other arithmetic, invert_factor(): factor = jnp.linalg.cholesky(b_full)  78.9 us
    another operation x3, other arithmetic, invert_factor(): return jax.scipy.linalg.solve_triangular(factor, identity, lower=True)  40.3 us
    all_to_all x1, waiting for transfers between devices, from_everyone(): return lax.all_to_all(copies, axis, split_axis=0, concat_axis=0, tiled=True)  24.4 us
    all_to_all x1, blocking collectives, gather_in_order(): lax.all_to_all(jnp.stack([pieces] * lax.axis_size(axes[k])), axes[k], 0, 0)  13 us
    all_to_all x1, waiting for transfers between devices, gather_in_order(): lax.all_to_all(jnp.stack([pieces] * lax.axis_size(axes[k])), axes[k], 0, 0)  11.1 us
  transfers between devices with their start and end apart: 4, of which 4 were waited for; matrix products, arithmetic and copies ran while one was open for 0% of the time, Pallas kernels for 0%

profile of v1, /device:TPU:8, one launch (start us, length us, event | category | flops | bytes accessed | tf_op | source)
XLA Modules:
  0.0 514.0 jit_solution(2227055183103803555)
XLA Ops:
  7.2 2.0 broadcast_in_dim.5
  9.1 8.5 %all-to-all-start = ((f32[16,32,512]{2,1,0:T(8,128)}), f32[16,32,512]{2,1,0:T(8,128)S(1)}, u32[]{:S(2)}, u32[]{:S(2)}) async-start(f32[16,32,512]{2,1,0:T(8,128)} %broadcast_in_dim.5), calls=%async_computation | async-start | bytes 2097152 | tf_op jit(solution)/shard_map/all_to_all | solution.py:20
  17.6 0.1 iota_compare_fusion
  17.7 0.1 fusion.10
  17.8 24.4 %all-to-all-done = f32[16,32,512]{2,1,0:T(8,128)S(1)} async-done(((f32[16,32,512]{2,1,0:T(8,128)}), f32[16,32,512]{2,1,0:T(8,128)S(1)}, u32[]{:S(2)}, u32[]{:S(2)}) %all-to-all-start) | async-done | bytes 1048608 | tf_op jit(solution)/shard_map/all_to_all | solution.py:20
  42.2 0.3 copy.12
  42.6 0.2 fusion.1
  42.8 1.0 copy-done.2
  43.8 11.7 %cholesky.104 = f32[128,128]{1,0:T(8,128)S(1)} custom-call(f32[128,128]{1,0:T(8,128)S(1)} %cholesky.266), custom_call_target="Cholesky" | custom-call | tf_op jit(solution)/shard_map/jit(cholesky)/cholesky | solution.py:68
  55.6 9.8 %custom-call.31 = f32[1,128,128]{1,2,0:T(8,128)S(1)} custom-call(f32[1,128,128]{2,1,0:T(8,128)S(1)} %get-tuple-element.35), custom_call_target="InvertDiagBlocksLowerTriangular" | custom-call | tf_op jit(solution)/shard_map/jit(cholesky)/cholesky | solution.py:68
  65.4 0.1 cholesky.224
  65.5 1.2 constant_dynamic-update-slice_fusion.1
  66.7 1.3 convolution_subtract_fusion.3
  68.0 11.7 %cholesky.217 = f32[128,128]{1,0:T(8,128)S(1)} custom-call(f32[128,128]{1,0:T(8,128)S(1)} %cholesky.270), custom_call_target="Cholesky" | custom-call | tf_op jit(solution)/shard_map/jit(cholesky)/cholesky | solution.py:68
  79.8 10.2 %custom-call.32 = f32[1,128,128]{1,2,0:T(8,128)S(1)} custom-call(f32[1,128,128]{2,1,0:T(8,128)S(1)} %get-tuple-element.32), custom_call_target="InvertDiagBlocksLowerTriangular" | custom-call | tf_op jit(solution)/shard_map/jit(cholesky)/cholesky | solution.py:68
  90.0 0.3 convolution_dynamic-update-slice_fusion
  90.3 1.3 convolution_subtract_fusion.4
  91.6 11.7 %cholesky.238 = f32[128,128]{1,0:T(8,128)S(1)} custom-call(f32[128,128]{1,0:T(8,128)S(1)} %cholesky.275), custom_call_target="Cholesky" | custom-call | tf_op jit(solution)/shard_map/jit(cholesky)/cholesky | solution.py:68
  103.3 0.6 compare_reduce_fusion.1
  104.0 9.8 %custom-call.33 = f32[1,128,128]{1,2,0:T(8,128)S(1)} custom-call(f32[1,128,128]{2,1,0:T(8,128)S(1)} %get-tuple-element.29), custom_call_target="InvertDiagBlocksLowerTriangular" | custom-call | tf_op jit(solution)/shard_map/jit(cholesky)/cholesky | solution.py:68
  113.8 0.2 convolution_dynamic-update-slice_fusion.1
  114.0 1.2 convolution_subtract_fusion.5
  115.2 11.7 %cholesky.255 = f32[128,128]{1,0:T(8,128)S(1)} custom-call(f32[128,128]{1,0:T(8,128)S(1)} %convolution_subtract_fusion.5), custom_call_target="Cholesky" | custom-call | tf_op jit(solution)/shard_map/jit(cholesky)/cholesky | solution.py:68
  127.0 0.6 compare_reduce_fusion
  127.6 0.8 compare_reduce_fusion.2
  130.9 0.1 select_select_fusion
  131.1 10.4 %while.1 = (s32[]{:T(128)}, f32[512,512]{1,0:T(8,128)S(1)}, s32[4,2]{0,1:T(2,128)S(1)}, f32[4,128,128]{2,1,0:T(8,128)}, s32[]{:T(128)}) while((s32[]{:T(128)}, f32[512,512]{1,0:T(8,128)S(1)}, s32[4,2]{0,1:T(2,128)S(1)}, f32[4,128,128]{2,1,0:T(8,128)}, s32[]{:T(128)}) %tuple.33), condition=%wide.while_cond, body=%wide.while_body.sunk | while | flops 2 | bytes 132205 | solution.py:70
  131.1 0.1 constant_dynamic-slice_fusion.3
  131.2 0.5 fusion.54
  131.7 2.0 bitcast_dynamic-update-slice_fusion.2
  133.8 0.5 fusion.54
  134.3 2.0 bitcast_dynamic-update-slice_fusion.2
  136.4 0.5 fusion.54
  136.9 2.0 bitcast_dynamic-update-slice_fusion.2
  139.0 0.5 fusion.54
  139.5 2.0 bitcast_dynamic-update-slice_fusion.2
  141.5 40.1 %custom-call.34 = f32[4,128,128]{1,2,0:T(8,128)S(1)} custom-call(f32[4,128,128]{2,1,0:T(8,128)} %get-tuple-element.11), custom_call_target="InvertDiagBlocksLowerTriangular" | custom-call | tf_op jit(solution)/shard_map/jit(_solve_triangular)/triangular_solve | solution.py:70
  181.7 0.3 fusion.12
  182.0 0.4 convolution_subtract_fusion.1
  182.4 0.4 fusion.24
  182.8 0.4 convolution_subtract_fusion
  183.2 0.4 fusion.22
  183.7 0.6 convolution_subtract_fusion.2
  184.3 1.3 fusion.21
  185.6 1.1 convolution_bitcast_fusion.1
  186.7 13.0 %all_to_all.15 = f32[4,1,32,512]{3,2,1,0:T(8,128)S(1)} all-to-all(f32[4,1,32,512]{3,2,1,0:T(8,128)S(1)} %stack.6), channel_id=1, replica_groups=mesh['row_0'=4,'row_1'=4,'col'=32] {'row_0'}, dimensions={0} | all-to-all | bytes 524288 | tf_op jit(solution)/shard_map/all_to_all | solution.py:31
  199.7 1.1 stack.7
  200.8 3.5 all-to-all-start.2
  204.4 1.1 fusion.35
  205.5 11.1 %all-to-all-done.2 = f32[4,4,32,512]{3,2,1,0:T(8,128)S(1)} async-done(((f32[4,4,32,512]{3,2,1,0:T(8,128)}), f32[4,4,32,512]{3,2,1,0:T(8,128)S(1)}, u32[]{:S(2)}, u32[]{:S(2)}) %all-to-all-start.2) | async-done | bytes 1048608 | tf_op jit(solution)/shard_map/all_to_all | solution.py:31
  216.6 0.1 copy.13
  216.7 1.9 fusion.36
  218.6 0.7 convolution_multiply_fusion
  219.3 1.7 fusion.39
  221.0 0.7 pad_maximum_fusion.1
  221.7 0.3 all-reduce.4.cloned.1.call-start
  222.0 95.5 %all-gather.2.cloned.1.call-done = f32[1024,1024]{1,0:T(8,128)} async-done(((f32[32,1024]{1,0:T(8,128)}), f32[1024,1024]{1,0:T(8,128)}) %all-gather.2.cloned.1.call-update) | async-done | bytes 4194320 | tf_op jit(solution)/shard_map/all_gather | solution.py:49
  317.5 2.7 fusion.38
  320.1 1.2 dynamic-slice_select_fusion
  321.3 1.1 dynamic-slice_select_fusion.1
  322.4 0.6 constant_dynamic-slice_fusion.1
  323.1 173.4 %all-reduce.4.cloned.1.call-done = (f32[512,512]{1,0:T(8,128)}, f32[512,512]{1,0:T(8,128)}) async-done(((f32[512,512]{1,0:T(8,128)}, f32[512,512]{1,0:T(8,128)}), (f32[512,512]{1,0:T(8,128)}, f32[512,512]{1,0:T(8,128)})) %all-reduce.4.cloned.1.call-update) | async-done | bytes 2097168 | tf_op jit(solution)/shard_map/psum | solution.py:54
  496.4 5.5 %fusion.33 = f32[1024,512]{1,0:T(8,128)S(1)} fusion(f32[512,512]{1,0:T(8,128)} %get-tuple-element.20, f32[1024,1024]{1,0:T(8,128)} %all-gather.2.cloned.1.call-done), kind=kOutput, calls=%fused_computation.78 | convolution fusion | flops 3221225472 | bytes 5242880 | tf_op jit(solution)/shard_map/dot_general | solution.py:62
  501.9 5.0 subtract_subtract_fusion
  (34 shorter events, 0.5 us)
Async XLA Ops:
  7.2 212.1 %copy-start = (f32[32,512]{1,0:T(8,128)S(1)}, f32[32,512]{1,0:T(8,128)}, u32[]{:S(2)}) copy-start(f32[32,512]{1,0:T(8,128)} %param.8) | copy-start | bytes 196612
  9.1 33.1 %all-to-all-start = ((f32[16,32,512]{2,1,0:T(8,128)}), f32[16,32,512]{2,1,0:T(8,128)S(1)}, u32[]{:S(2)}, u32[]{:S(2)}) async-start(f32[16,32,512]{2,1,0:T(8,128)} %broadcast_in_dim.5), calls=%async_computation | async-start | bytes 2097152 | tf_op jit(solution)/shard_map/all_to_all | solution.py:20
  42.8 1.0 copy-start.2
  181.7 1.6 copy-start.5
  182.4 3.2 copy-start.7
  186.7 17.7 %copy-start.8 = (f32[32,512]{1,0:T(8,128)S(1)}, f32[32,512]{1,0:T(8,128)}, u32[]{:S(2)}) copy-start(f32[32,512]{1,0:T(8,128)} %param.7) | copy-start | bytes 196612
  200.8 15.8 %all-to-all-start.2 = ((f32[4,4,32,512]{3,2,1,0:T(8,128)}), f32[4,4,32,512]{3,2,1,0:T(8,128)S(1)}, u32[]{:S(2)}, u32[]{:S(2)}) async-start(f32[4,4,32,512]{3,2,1,0:T(8,128)} %stack.7), calls=%async_computation.2 | async-start | bytes 2097152 | tf_op jit(solution)/shard_map/all_to_all | solution.py:31
  204.4 113.1 %all-gather.2.cloned.1.call-start = ((), (), s32[]{:S(2)}) async-start(), calls=%async_computation.3 | async-start | bytes 4325376 | tf_op jit(solution)/shard_map/all_gather | solution.py:49
  205.5 15.5 %copy-start.6 = (f32[512,32]{0,1:T(8,128)}, f32[512,32]{0,1:T(8,128)S(1)}, u32[]{:S(2)}) copy-start(f32[512,32]{0,1:T(8,128)S(1)} %fusion.35) | copy-start | bytes 196612
  221.7 274.7 %all-reduce.4.cloned.1.call-start = ((), (), s32[]{:S(2)}) async-start(), calls=%async_computation.4 | async-start | bytes 4194304 | tf_op jit(solution)/shard_map/psum | solution.py:54
  322.4 179.5 %copy-start.3 = (f32[1024,512]{1,0:T(8,128)S(1)}, f32[1024,512]{1,0:T(8,128)}, u32[]{:S(2)}) copy-start(f32[1024,512]{1,0:T(8,128)} %param.9) | copy-start | bytes 6291460
  496.4 5.5 %copy-start.1 = (f32[1024,1024]{1,0:T(8,128)S(1)}, f32[1024,1024]{1,0:T(8,128)}, u32[]{:S(2)}) copy-start(f32[1024,1024]{1,0:T(8,128)} %all-gather.2.cloned.1.call-done) | copy-start | bytes 12582916
  496.4 5.5 %copy-start.4 = (f32[512,512]{1,0:T(8,128)S(1)}, f32[512,512]{1,0:T(8,128)}, u32[]{:S(2)}) copy-start(f32[512,512]{1,0:T(8,128)} %get-tuple-element.21) | copy-start | bytes 3145732
Sparse Core Ops, SparseCore 0:
  221.8 95.5 all-gather.1
  322.6 173.8 all-reduce.3
